TPU v7x, 512 devices: a whole 4x8x8 slice. The times are simulated.
512 devices in a mesh: group: 16 (over z_hi, x, core), blk: 32 (over z_lo, y).
Axes of the slice: x: 4, y: 8, z: 8 (z_hi: 2, z_lo: 4; z = z_hi * 4 + z_lo), core: 2. Of those that a mesh axis runs over, the one named last changes fastest.
Arguments:
- teacher: bfloat16 [65536, 1024], P(('group', 'blk')), may hold values from -300 to 300
- student: bfloat16 [65536, 768], P(('group', 'blk')), may hold values from -300 to 300
Outputs:
- student_grad: float32 [65536, 768], P(('group', 'blk'))
- mean_loss: float32 [], replicated
All inputs are finite; a program needn't handle non-finite values.
Results may differ from a plain program's by a relative error of at most 0.039.
Values may be sent and summed in bfloat16 or wider, within the bound.
A program may use at most 64 MiB of HBM per device.

v0:
```python
import jax
import jax.numpy as jnp
from jax import lax
from jax.sharding import PartitionSpec as P


def block_distance(left_rows, right_rows):
    left_norm = jnp.sum(jnp.square(left_rows.astype(jnp.float32)), 1)
    right_norm = jnp.sum(jnp.square(right_rows.astype(jnp.float32)), 1)
    products = lax.dot_general(
        left_rows, right_rows, (((1,), (1,)), ((), ())), preferred_element_type=jnp.float32
    )
    spread = left_norm[:, None] + right_norm[None, :] - 2.0 * products
    return jnp.sqrt(jnp.maximum(spread, 0.0) + 1.0)


def pair_weights(dist_student, dist_teacher, weight, pair_count):
    total_student, total_teacher = lax.psum(
        (jnp.sum(weight * dist_student), jnp.sum(weight * dist_teacher)), ("group", "blk")
    )
    mean_student = total_student / pair_count
    mean_teacher = total_teacher / pair_count
    errors = dist_student / mean_student - dist_teacher / mean_teacher
    slopes = jnp.clip(errors, -1.0, 1.0)
    huber_terms = jnp.where(jnp.abs(errors) < 1.0, 0.5 * errors * errors, jnp.abs(errors) - 0.5)
    curvature, huber_sum = lax.psum(
        (jnp.sum(weight * slopes * dist_student), jnp.sum(weight * huber_terms)), ("group", "blk")
    )
    factor = curvature / (pair_count * mean_student * mean_student)
    weights = jnp.where(weight > 0.0, (slopes / mean_student - factor) / dist_student, 0.0).astype(
        jnp.bfloat16
    )
    return (weights, huber_sum / pair_count)


def shards(teacher, student):
    rows_dev = student.shape[0]
    blocks = lax.axis_size("blk")
    batch_rows = rows_dev * blocks
    pair_count = 1.0 * lax.axis_size("group") * batch_rows * (batch_rows - 1)
    student_wide = student.astype(jnp.float32)
    pieces = (
        lax.all_gather(teacher, "blk", axis=0, tiled=True),
        lax.all_gather(student, "blk", axis=0, tiled=True),
    )
    dist_teacher = block_distance(teacher, pieces[0])
    dist_student = block_distance(student, pieces[1])
    stored = pieces[1]
    dist_teacher, dist_student, stored = (dist_teacher, dist_student, stored)
    own_index = lax.axis_index("blk") * rows_dev + jnp.arange(rows_dev)
    weight = (own_index[:, None] != jnp.arange(batch_rows)[None, :]).astype(jnp.float32)
    weights, mean_loss = pair_weights(dist_student, dist_teacher, weight, pair_count)
    row_total = jnp.sum(weights.astype(jnp.float32), 1)
    gradient = student_wide * row_total[:, None] - jnp.dot(
        weights, stored, preferred_element_type=jnp.float32
    )
    return (gradient, mean_loss)


def solution(mesh):
    in_specs = (P(("group", "blk"), None), P(("group", "blk"), None))
    out_specs = (P(("group", "blk"), None), P())
    return jax.shard_map(shards, mesh=mesh, in_specs=in_specs, out_specs=out_specs, check_vma=False)
```

profile of v0, /device:TPU:1, one launch (start us, length us, event | category | flops | bytes accessed | tf_op | source)
XLA Modules:
  0.0 574.4 jit_solution(7632110732589659440)
XLA Ops:
  7.2 0.0 all-gather.3.cloned.1.call-start
  7.2 0.7 all-gather.3.cloned.1.call-update
  7.9 0.0 all-gather.5.cloned.1.call-start
  7.9 0.7 all-gather.5.cloned.1.call-update
  8.7 1.0 fusion.11
  9.7 1.1 multiply_reduce_fusion.3
  10.8 150.5 %all-gather.3.cloned.1.call-done = bf16[4096,768]{1,0:T(8,128)(2,1)} async-done(((bf16[128,768]{1,0:T(8,128)(2,1)}), bf16[4096,768]{1,0:T(8,128)(2,1)}) %all-gather.3.cloned.1.call-update) | async-done | bytes 6291472 | tf_op jit(solution)/shard_map/all_gather | solution.py:44
  161.3 0.0 copy-start.2
  161.3 4.1 multiply_reduce_fusion.1
  165.4 162.5 %all-gather.5.cloned.1.call-done = bf16[4096,1024]{1,0:T(8,128)(2,1)} async-done(((bf16[128,1024]{1,0:T(8,128)(2,1)}), bf16[4096,1024]{1,0:T(8,128)(2,1)}) %all-gather.5.cloned.1.call-update) | async-done | bytes 8388624 | tf_op jit(solution)/shard_map/all_gather | solution.py:43
  327.9 0.0 copy-start
  327.9 5.2 multiply_reduce_fusion
  333.1 0.0 copy-done.2
  333.1 0.5 copy-done
  333.6 0.0 copy-start.1
  333.6 0.0 copy-start.3
  333.6 3.4 fusion.7
  337.0 0.0 copy-done.1
  337.0 0.0 copy-done.3
  337.1 4.5 select_reduce_fusion.1
  341.5 116.2 %all-reduce.1 = (f32[]{:T(128)}, f32[]{:T(128)}) all-reduce(f32[]{:T(128)} %get-tuple-element.5, f32[]{:T(128)} %get-tuple-element.4), channel_id=1, replica_groups=mesh['group'=16,'blk'=32] {'group','blk'}, use_global_device_ids=true, to_apply=%region_7.0 | all-reduce | flops 2 | bytes 16 | tf_op jit(solution)/shard_map/psum | solution.py:18
  459.7 3.3 fusion.10
  463.0 94.8 %all-reduce = (f32[]{:T(128)}, f32[]{:T(128)}) all-reduce(f32[]{:T(128)} %get-tuple-element.3, f32[]{:T(128)} %get-tuple-element.2), channel_id=1, replica_groups=mesh['group'=16,'blk'=32] {'group','blk'}, use_global_device_ids=true, to_apply=%region_9.10 | all-reduce | flops 2 | bytes 16 | tf_op jit(solution)/shard_map/psum | solution.py:26
  558.5 2.7 convert_reduce_fusion
  561.9 4.5 convolution_subtract_fusion
  (1 shorter events, 0.0 us)
Async XLA Ops:
  7.2 154.1 %all-gather.3.cloned.1.call-start = ((), (), s32[]{:S(2)}) async-start(), calls=%async_computation | async-start | bytes 6488064 | tf_op jit(solution)/shard_map/all_gather | solution.py:44
  7.9 320.0 %all-gather.5.cloned.1.call-start = ((), (), s32[]{:S(2)}) async-start(), calls=%async_computation.1 | async-start | bytes 8650752 | tf_op jit(solution)/shard_map/all_gather | solution.py:43
  161.3 171.9 %copy-start.2 = (bf16[128,1024]{1,0:T(8,128)(2,1)S(1)}, bf16[128,1024]{1,0:T(8,128)(2,1)}, u32[]{:S(2)}) copy-start(bf16[128,1024]{1,0:T(8,128)(2,1)} %param.2) | copy-start | bytes 786436
  327.9 5.8 %copy-start = (bf16[4096,1024]{1,0:T(8,128)(2,1)S(1)}, bf16[4096,1024]{1,0:T(8,128)(2,1)}, u32[]{:S(2)}) copy-start(bf16[4096,1024]{1,0:T(8,128)(2,1)} %all-gather.5.cloned.1.call-done) | copy-start | bytes 25165828
  333.6 3.4 copy-start.1
  333.6 3.4 copy-start.3
Sparse Core Ops, SparseCore 0:
  10.1 151.1 all-gather.2
  163.3 164.4 all-gather.4
where the time goes:
time: 575 us; the launch traced here: 574 us
  waiting for transfers between devices  314 us (55%)
  blocking collectives  211 us (37%)
  between operations  18.5 us (3%)
  other arithmetic  17.5 us (3%)
  matrix products  12.4 us (2%)
    all_gather x1, waiting for transfers between devices, shards(): lax.all_gather(teacher, 'blk', axis=0, tiled=True)  162 us
    all_gather x1, waiting for transfers between devices, shards(): lax.all_gather(student, 'blk', axis=0, tiled=True)  150 us
    psum x1, blocking collectives, pair_weights(): lax.psum((jnp.sum(weight * dist_student), jnp.sum(weight * dist_teacher))...  116 us
    psum x1, blocking collectives, pair_weights(): lax.psum((jnp.sum(weight * slopes * dist_student), jnp.sum(weight * huber...  94.8 us
  transfers between devices with their start and end apart: 2, of which 2 were waited for; matrix products, arithmetic and copies ran while one was open for 1% of the time, Pallas kernels for 0%

commit v1 on v0

v1 whole, which is shorter than its diff:
```python
import functools
import jax
import jax.numpy as jnp
from jax import lax
from jax.experimental import pallas as pl
from jax.experimental.pallas import tpu as pltpu
from jax.sharding import PartitionSpec as P

MESH = pl.DeviceIdType.MESH
F32 = jnp.float32
NY = 8
NZ = 4
NP = 8
NT = (((1,), (1,)), ((), ()))


def fold(values):
    rows, columns = values.shape
    part = jnp.sum(values.reshape(rows // 8, 8, columns), 0)
    total = part[:, 0:128]
    for k in range(1, columns // 128):
        total = total + part[:, k * 128 : (k + 1) * 128]
    return total


def kernel(
    pair_count,
    t_ref, s_ref, grad_ref, loss_ref,
    ti, si, tj, sj,
    dist_t, dist_s, inv_s, norm_t, norm_s,
    w_ij, w_ji, part_i, part_j,
    in_yr, in_yl, in_zr, in_zl,
    sums,
    send_y, recv_y, send_z, recv_z,
    send_sum, recv_sum,
    send_gy, recv_gy, send_gz, recv_gz,
):
    rows, dt = t_ref.shape
    ds = s_ref.shape[1]
    half = rows // 2
    cut = part_j.shape[1]
    group = lax.axis_index("group")
    blk = lax.axis_index("blk")
    b, c = blk // NY, lax.rem(blk, NY)
    core, rest = lax.rem(group, 2), group // 2
    zc = b * 2 + core

    def y_device(index):
        return (group, b * NY + index)

    def zc_device(index):
        return (rest * 2 + lax.rem(index, 2), (index // 2) * NY + c)

    def rest_device(index):
        return (index * 2 + core, blk)

    stages = ((y_device, c), (zc_device, zc), (rest_device, rest))

    barrier = pltpu.get_barrier_semaphore()
    for device, me in stages:
        for j in range(1, NP):
            pl.semaphore_signal(
                barrier, inc=1, device_id=device(lax.rem(me + j, NP)), device_id_type=MESH
            )
    ti[0:rows] = t_ref[...]
    si[0:rows] = s_ref[...]
    tj[0:rows] = t_ref[...]
    sj[0:rows] = s_ref[...]
    pl.semaphore_wait(barrier, 3 * (NP - 1))

    y_right, y_left = y_device(lax.rem(c + 1, NY)), y_device(lax.rem(c + NY - 1, NY))
    z_right = (group, lax.rem(blk + NY, NY * NZ))
    z_left = (group, lax.rem(blk + NY * (NZ - 1), NY * NZ))

    def slot(k):
        return pl.ds(k * rows, rows)

    def y_copy(what, src, dst, to):
        ref = (si, ti)[what]
        return pltpu.make_async_remote_copy(
            src_ref=ref.at[slot(src)], dst_ref=ref.at[slot(dst)],
            send_sem=send_y.at[what, dst], recv_sem=recv_y.at[what, dst],
            device_id=to, device_id_type=MESH,
        )

    def z_copy(what, src, dst, to, way):
        ref = (sj, tj)[what]
        return pltpu.make_async_remote_copy(
            src_ref=ref.at[slot(src)], dst_ref=ref.at[slot(dst)],
            send_sem=send_z.at[what, way, dst], recv_sem=recv_z.at[what, dst],
            device_id=to, device_id_type=MESH,
        )

    def z_wait(what, dst):
        z_copy(what, 0, dst, z_right, 0).wait_recv()

    for what in range(2):
        y_copy(what, 0, 7, y_right).start()
        y_copy(what, 0, 1, y_left).start()

        @pl.when(b < 3)
        def _():
            z_copy(what, 0, 3, z_right, 0).start()

        @pl.when(b > 0)
        def _():
            z_copy(what, 0, 1, z_left, 1).start()

    for what in range(2):
        y_copy(what, 0, 7, y_right).wait_recv()
        y_copy(what, 7, 6, y_right).start()
        y_copy(what, 0, 1, y_left).wait_recv()
        y_copy(what, 1, 2, y_left).start()

        @pl.when(b >= 1)
        def _():
            z_wait(what, 3)

        @pl.when((b >= 1) & (b < 3))
        def _():
            z_copy(what, 3, 2, z_right, 0).start()

        @pl.when(b <= 2)
        def _():
            z_wait(what, 1)

        @pl.when((b <= 2) & (b > 0))
        def _():
            z_copy(what, 1, 2, z_left, 1).start()

    for what in range(2):
        y_copy(what, 7, 6, y_right).wait_recv()
        y_copy(what, 6, 5, y_right).start()
        y_copy(what, 1, 2, y_left).wait_recv()
        y_copy(what, 2, 3, y_left).start()
        z_wait(what, 2)

        @pl.when(b == 2)
        def _():
            z_copy(what, 2, 1, z_right, 0).start()

        @pl.when(b == 1)
        def _():
            z_copy(what, 2, 3, z_left, 1).start()

    y_copy(0, 2, 3, y_left).wait_recv()
    y_copy(0, 3, 4, y_left).start()
    y_copy(0, 6, 5, y_right).wait_recv()
    y_copy(1, 6, 5, y_right).wait_recv()
    y_copy(1, 5, 4, y_right).start()
    y_copy(1, 2, 3, y_left).wait_recv()

    for what in range(2):

        @pl.when(b == 0)
        def _():
            z_wait(what, 3)

        @pl.when(b == 3)
        def _():
            z_wait(what, 1)

    for ref, norm in ((tj, norm_t), (sj, norm_s)):
        for k in range(NZ):
            wide = ref[slot(k)].astype(F32)
            squares = jnp.sum(wide * wide, 1, keepdims=True)
            turned = jnp.transpose(jnp.broadcast_to(squares, (rows, 128)))
            norm[:, k * rows : (k + 1) * rows] = turned[0:8]

    def distance(ref, other, norm, place):
        own = ref[place]
        wide = own.astype(F32)
        squares = jnp.sum(wide * wide, 1, keepdims=True)
        products = lax.dot_general(own, other[...], NT, preferred_element_type=F32)
        spread = squares + norm[0:1] - 2.0 * products
        return jnp.sqrt(jnp.maximum(spread, 0.0) + 1.0)

    def first_pass(k, diagonal):
        place = pl.ds(pl.multiple_of(k * rows, rows), rows)
        near_t = distance(ti, tj, norm_t, place)
        near_s = distance(si, sj, norm_s, place)
        inverse = 1.0 / near_s
        if diagonal:
            at = lax.broadcasted_iota(jnp.int32, near_s.shape, 0)
            off = at != lax.broadcasted_iota(jnp.int32, near_s.shape, 1)
            near_t = jnp.where(off, near_t, 0.0)
            near_s = jnp.where(off, near_s, 0.0)
            inverse = jnp.where(off, inverse, 0.0)
        dist_t[place] = near_t
        dist_s[place] = near_s
        inv_s[place] = inverse
        return fold(near_s), fold(near_t)

    def add_pass(total, more):
        return total[0] + more[0], total[1] + more[1]

    total = first_pass(0, True)
    total = lax.fori_loop(1, 4, lambda k, now: add_pass(now, first_pass(k, False)), total)
    total = lax.fori_loop(5, 8, lambda k, now: add_pass(now, first_pass(k, False)), total)
    y_copy(0, 3, 4, y_left).wait_recv()
    y_copy(1, 5, 4, y_right).wait_recv()
    total = add_pass(total, first_pass(4, False))

    def sum_all(which, pair):
        one, two = (jnp.sum(tile, 0, keepdims=True) for tile in pair)
        first = lax.broadcasted_iota(jnp.int32, (8, 128), 0) == 0
        tile = jnp.where(first, one, two)
        for stage, (device, me) in enumerate(stages):
            at = which * 3 + stage
            sums[at, me] = tile

            def copy(j):
                return pltpu.make_async_remote_copy(
                    src_ref=sums.at[at, me], dst_ref=sums.at[at, me],
                    send_sem=send_sum.at[at, j], recv_sem=recv_sum.at[at, me],
                    device_id=device(lax.rem(me + j, NP)), device_id_type=MESH,
                )

            for j in range(1, NP):
                copy(j).start()
            for j in range(1, NP):
                peer = lax.rem(me + j, NP)
                pltpu.make_async_remote_copy(
                    src_ref=sums.at[at, peer], dst_ref=sums.at[at, peer],
                    send_sem=send_sum.at[at, j], recv_sem=recv_sum.at[at, peer],
                    device_id=device(peer), device_id_type=MESH,
                ).wait_recv()
            tile = sums[at, 0]
            for j in range(1, NP):
                tile = tile + sums[at, j]
            for j in range(1, NP):
                copy(j).wait_send()
        wide = jnp.sum(tile, 1, keepdims=True)
        return wide[0:1], wide[1:2]

    total_s, total_t = sum_all(0, total)
    scale_s = pair_count / total_s
    scale_t = pair_count / total_t

    def second_pass(k, now):
        place = pl.ds(pl.multiple_of(k * rows, rows), rows)
        near_s = dist_s[place]
        error = near_s * scale_s - dist_t[place] * scale_t
        slope = jnp.clip(error, -1.0, 1.0)
        dist_t[place] = slope
        return now[0] + fold(slope * near_s), now[1] + fold(slope * (error - 0.5 * slope))

    zero = jnp.zeros((8, 128), F32)
    curvature, huber = sum_all(1, lax.fori_loop(0, NY, second_pass, (zero, zero)))
    loss_ref[...] = jnp.broadcast_to(huber / pair_count, (8, 128))
    factor = curvature * scale_s * scale_s / pair_count

    def third_pass(k, carry):
        start = pl.multiple_of(k * rows, rows)
        place = pl.ds(start, rows)
        weight = (dist_t[place] * scale_s - factor) * inv_s[place]
        w_ij[place] = weight.astype(jnp.bfloat16)
        w_ji[:, place] = jnp.transpose(weight).astype(jnp.bfloat16)
        return carry

    lax.fori_loop(0, NY, third_pass, 0)

    def make_i(k):
        weight = w_ij[slot(k)]
        count = jnp.sum(weight.astype(F32), 1, keepdims=True)
        part_i[slot(k)] = si[slot(k), cut:ds].astype(F32) * count - jnp.dot(
            weight, sj[:, cut:ds], preferred_element_type=F32
        )

    def make_j(k):
        weight = w_ji[slot(k)]
        count = jnp.sum(weight.astype(F32), 1, keepdims=True)
        part_j[slot(k)] = sj[slot(k), 0:cut].astype(F32) * count - jnp.dot(
            weight, si[:, 0:cut], preferred_element_type=F32
        )

    def gy_copy(way, m, piece):
        k = m if way == 0 else (NY - m) % NY
        return pltpu.make_async_remote_copy(
            src_ref=part_i.at[pl.ds(k * rows + piece * half, half)],
            dst_ref=(in_yr, in_yl)[way].at[m - 1, piece],
            send_sem=send_gy.at[way, m - 1, piece], recv_sem=recv_gy.at[way, m - 1, piece],
            device_id=(y_right, y_left)[way], device_id_type=MESH,
        )

    def gy_add(way, m, piece):
        gy_copy(way, m + 1, piece).wait_recv()
        k = m if way == 0 else (NY - m) % NY
        place = pl.ds(k * rows + piece * half, half)
        part_i[place] = part_i[place] + (in_yr, in_yl)[way][m, piece]

    def gz_copy(way, m, piece):
        k = m if way == 0 else (NZ - m) % NZ
        return pltpu.make_async_remote_copy(
            src_ref=part_j.at[pl.ds(k * rows + piece * half, half)],
            dst_ref=(in_zr, in_zl)[way].at[m - 1, piece],
            send_sem=send_gz.at[way, m - 1, piece], recv_sem=recv_gz.at[way, m - 1, piece],
            device_id=(z_right, z_left)[way], device_id_type=MESH,
        )

    def gz_add(way, m, piece):
        gz_copy(way, m + 1, piece).wait_recv()
        k = m if way == 0 else (NZ - m) % NZ
        place = pl.ds(k * rows + piece * half, half)
        part_j[place] = part_j[place] + (in_zr, in_zl)[way][m, piece]

    def gz_sends(way, m):
        sends = (b + m <= NZ - 1) if way == 0 else (b - m >= 0)
        comes = (b >= 1) if way == 0 else (b <= NZ - 2)
        return sends, sends & comes

    def gz_round(m, add):
        for piece in range(2):
            for way in range(2):
                sends, comes = gz_sends(way, m)
                if add:

                    @pl.when(comes)
                    def _():
                        gz_add(way, m, piece)

                @pl.when(sends)
                def _():
                    gz_copy(way, m, piece).start()

    make_i(4)
    gy_copy(0, 4, 0).start()
    gy_copy(1, 4, 1).start()
    make_j(3)
    make_j(1)
    gz_round(3, False)
    make_i(3)
    make_i(5)
    gy_copy(0, 3, 1).start()
    gy_copy(1, 3, 0).start()
    make_j(2)
    make_i(2)
    make_i(6)
    make_i(1)
    make_i(7)
    make_i(0)
    make_j(0)

    gy_add(0, 3, 0)
    gy_copy(0, 3, 0).start()
    gy_add(1, 3, 1)
    gy_copy(1, 3, 1).start()
    gz_round(2, True)
    for m in (2, 1):
        for piece in range(2):
            for way in range(2):
                order = 1 - piece if way == 0 else piece
                gy_add(way, m, order)
                gy_copy(way, m, order).start()
        if m == 2:
            gz_round(1, True)

    for piece in range(2):
        for way in range(2):
            sends, comes = gz_sends(way, 0)

            @pl.when(comes)
            def _():
                gz_add(way, 0, piece)

    for piece in range(2):
        for way in range(2):
            gy_add(way, 0, 1 - piece if way == 0 else piece)
    grad_ref[:, 0:cut] = part_j[0:rows]
    grad_ref[:, cut:ds] = part_i[0:rows]

    for what in range(2):
        for src, dst, to in ((0, 7, y_right), (0, 1, y_left), (7, 6, y_right), (1, 2, y_left),
                             (6, 5, y_right), (2, 3, y_left)):
            y_copy(what, src, dst, to).wait_send()
        for cond, src, dst, to, way in (
            (b < 3, 0, 3, z_right, 0), (b > 0, 0, 1, z_left, 1),
            ((b >= 1) & (b < 3), 3, 2, z_right, 0), ((b <= 2) & (b > 0), 1, 2, z_left, 1),
            (b == 2, 2, 1, z_right, 0), (b == 1, 2, 3, z_left, 1),
        ):

            @pl.when(cond)
            def _():
                z_copy(what, src, dst, to, way).wait_send()

    y_copy(0, 3, 4, y_left).wait_send()
    y_copy(1, 5, 4, y_right).wait_send()
    for way in range(2):
        gy_copy(way, 4, way).wait_send()
        for m in (3, 2, 1):
            for piece in range(2):
                gy_copy(way, m, piece).wait_send()
            sends, _ = gz_sends(way, m)

            @pl.when(sends)
            def _():
                for piece in range(2):
                    gz_copy(way, m, piece).wait_send()


def shards(teacher, student):
    rows, dt = teacher.shape
    ds = student.shape[1]
    batch_rows = rows * lax.axis_size("blk")
    pair_count = 1.0 * lax.axis_size("group") * batch_rows * (batch_rows - 1)
    cut = ds // 2
    ni, nj = NY * rows, NZ * rows
    bf16 = jnp.bfloat16
    vmem, dma = pltpu.VMEM, pltpu.SemaphoreType.DMA
    gradient, loss = pl.pallas_call(
        functools.partial(kernel, pair_count),
        out_shape=(
            jax.ShapeDtypeStruct((rows, ds), F32),
            jax.ShapeDtypeStruct((8, 128), F32),
        ),
        in_specs=[pl.BlockSpec(memory_space=vmem)] * 2,
        out_specs=[pl.BlockSpec(memory_space=vmem)] * 2,
        scratch_shapes=[
            vmem((ni, dt), bf16), vmem((ni, ds), bf16), vmem((nj, dt), bf16), vmem((nj, ds), bf16),
            vmem((ni, nj), F32), vmem((ni, nj), F32), vmem((ni, nj), F32),
            vmem((8, nj), F32), vmem((8, nj), F32),
            vmem((ni, nj), bf16), vmem((nj, ni), bf16),
            vmem((ni, ds - cut), F32), vmem((nj, cut), F32),
            vmem((4, 2, rows // 2, ds - cut), F32), vmem((4, 2, rows // 2, ds - cut), F32),
            vmem((3, 2, rows // 2, cut), F32), vmem((3, 2, rows // 2, cut), F32),
            vmem((6, NP, 8, 128), F32),
            dma((2, NY)), dma((2, NY)), dma((2, 2, NZ)), dma((2, NZ)),
            dma((6, NP)), dma((6, NP)),
            dma((2, 4, 2)), dma((2, 4, 2)), dma((2, 3, 2)), dma((2, 3, 2)),
        ],
        compiler_params=pltpu.CompilerParams(
            collective_id=0, has_side_effects=True, vmem_limit_bytes=50 * 1024 * 1024
        ),
    )(teacher, student)
    return (gradient, loss[0, 0])


def solution(mesh):
    in_specs = (P(("group", "blk"), None), P(("group", "blk"), None))
    out_specs = (P(("group", "blk"), None), P())
    return jax.shard_map(shards, mesh=mesh, in_specs=in_specs, out_specs=out_specs, check_vma=False)
```

time: 575 us -> 109 us (0.19)
  the two profiles are of different devices: /device:TPU:1 before, /device:TPU:16 now
where the time goes in v1:
time: 109 us
  Pallas kernels  105 us (96%)
  local copies, waits for them, and re-layouts  3.13 us (3%)
    pallas_call x1, Pallas kernels, shards(): pl.pallas_call(functools.partial(kernel, pair_count), out_shape=(jax.Shap...  105 us
    unnamed x5, local copies, waits for them, and re-layouts  2.61 us

profile of v1, /device:TPU:16, one launch (start us, length us, event | category | flops | bytes accessed | tf_op | source)
XLA Modules:
  0.0 108.6 jit_solution(815359251212594252)
XLA Ops:
  0.6 0.0 copy-start
  0.6 0.9 copy-done
  1.6 0.0 copy-start.1
  1.6 0.9 copy-done.1
  2.5 104.8 %shard_map.41 = (f32[128,768]{1,0:T(8,128)S(1)}, f32[8,128]{1,0:T(8,128)S(1)}) custom-call(bf16[128,1024]{1,0:T(8,128)(2,1)S(1)} %copy-done, bf16[128,768]{1,0:T(8,128)(2,1)S(1)} %copy-done.1), custom_call_target="tpu_custom_call" | custom-call | tf_op jit(solution)/shard_map/pallas_call | solution.py:410
  107.3 0.5 slice.3
  107.8 0.7 copy.5
Async XLA Ops:
  0.6 1.0 copy-start
  1.6 0.9 copy-start.1

commit v2 on v1

v2 whole, which is shorter than its diff:
```python
import functools
import jax
import jax.numpy as jnp
from jax import lax
from jax.experimental import pallas as pl
from jax.experimental.pallas import tpu as pltpu
from jax.sharding import PartitionSpec as P

MESH = pl.DeviceIdType.MESH
F32 = jnp.float32
NY = 8
NZ = 4
NX = 4
NP = 8
NT = (((1,), (1,)), ((), ()))


def fold(values):
    rows, columns = values.shape
    part = jnp.sum(values.reshape(rows // 8, 8, columns), 0)
    total = part[:, 0:128]
    for k in range(1, columns // 128):
        total = total + part[:, k * 128 : (k + 1) * 128]
    return total


def kernel(
    pair_count,
    t_ref, s_ref, grad_ref, loss_ref,
    ti, si, tj, sj,
    dist_t, dist_s, inv_s, norm_t, norm_s, own_t, own_s,
    w_ij, w_ji, part_i, part_j,
    in_yr, in_yl, in_zr, in_zl,
    sums,
    load, send_y, recv_y, send_z, recv_z,
    send_sum, recv_sum,
    send_gy, recv_gy, send_gz, recv_gz,
    inside,
):
    rows = t_ref.shape[0]
    ds = s_ref.shape[1]
    half = rows // 2
    cut = part_j.shape[1]
    group = lax.axis_index("group")
    blk = lax.axis_index("blk")
    b, c = blk // NY, lax.rem(blk, NY)
    core, x = lax.rem(group, 2), lax.rem(group // 2, NX)
    z = (group // (2 * NX)) * NZ + b
    xc = x * 2 + core

    def device(z, x, core, y):
        return ((z // NZ * NX + x) * 2 + core, lax.rem(z, NZ) * NY + y)

    def y_device(index):
        return device(z, x, core, index)

    def z_device(index):
        return device(index, x, core, c)

    def xc_device(index):
        return device(z, index // 2, lax.rem(index, 2), c)

    stages = ((y_device, c), (z_device, z), (xc_device, xc))

    y_right, y_left = y_device(lax.rem(c + 1, NY)), y_device(lax.rem(c + NY - 1, NY))
    z_right, z_left = z_device(lax.rem(z + 1, NP)), z_device(lax.rem(z + NP - 1, NP))
    near = (
        y_right, y_left, z_right, z_left,
        device(z, lax.rem(x + 1, NX), core, c), device(z, lax.rem(x + NX - 1, NX), core, c),
        device(z, x, 1 - core, c),
    )

    barrier = pltpu.get_barrier_semaphore()
    for other in near:
        pl.semaphore_signal(barrier, inc=1, device_id=other, device_id_type=MESH)

    def slot(k):
        return pl.ds(k * rows, rows)

    loads = [
        pltpu.make_async_copy(src, dst.at[slot(0)], load.at[n])
        for n, (src, dst) in enumerate(((s_ref, si), (s_ref, sj), (t_ref, ti), (t_ref, tj)))
    ]
    for copy in loads:
        copy.start()
    for copy in loads:
        copy.wait()
    pl.semaphore_wait(barrier, len(near))

    def round_signal(r):
        for other in near:
            pl.semaphore_signal(inside.at[r], inc=1, device_id=other, device_id_type=MESH)

    def round_wait(r):
        pl.semaphore_wait(inside.at[r], len(near))

    y_up = y_device(lax.rem(c + jnp.where(core == 0, 1, NY - 1), NY))
    y_down = y_device(lax.rem(c + jnp.where(core == 0, NY - 1, 1), NY))

    def piece_of(refs, k, piece):
        return refs[piece // 2].at[pl.ds(k * rows + (piece % 2) * half, half)]

    def y_copy(piece, src, dst, to):
        return pltpu.make_async_remote_copy(
            src_ref=piece_of((si, ti), src, piece), dst_ref=piece_of((si, ti), dst, piece),
            send_sem=send_y.at[piece, dst], recv_sem=recv_y.at[piece, dst],
            device_id=to, device_id_type=MESH,
        )

    def place(k, b):
        last = jnp.where(b == 0, 3, jnp.where(b == 3, 1, 2))
        return jnp.where(last == k, 3, last if k == 3 else k)

    def z_piece(k, b, piece):
        start = pl.multiple_of(place(k, b) * rows + (piece % 2) * half, half)
        return (sj, tj)[piece // 2].at[pl.ds(start, half)]

    def z_copy(piece, src, dst, to, way):
        return pltpu.make_async_remote_copy(
            src_ref=z_piece(src, b, piece), dst_ref=z_piece(dst, b + (1, -1)[way], piece),
            send_sem=send_z.at[piece, way, dst], recv_sem=recv_z.at[piece, dst],
            device_id=to, device_id_type=MESH,
        )

    def z_wait(piece, dst):
        pltpu.make_async_remote_copy(
            src_ref=z_piece(0, b, piece), dst_ref=z_piece(dst, b, piece),
            send_sem=send_z.at[piece, 0, dst], recv_sem=recv_z.at[piece, dst],
            device_id=z_right, device_id_type=MESH,
        ).wait_recv()

    def y_early(k):
        for piece in range(4):
            if k > 0:
                y_copy(piece, k - 1, k, y_down).wait_recv()
            if k < 4:
                y_copy(piece, k, k + 1, y_down).start()

    def y_late(k):
        for piece in range(4):
            if k > 0:
                y_copy(piece, (NY + 1 - k) % NY, NY - k, y_up).wait_recv()
            if k < 3:
                y_copy(piece, (NY - k) % NY, NY - k - 1, y_up).start()

    def z_step(k):
        for piece in range(4):
            if k == 0:

                @pl.when(b < 3)
                def _():
                    z_copy(piece, 0, 3, z_right, 0).start()

                @pl.when(b > 0)
                def _():
                    z_copy(piece, 0, 1, z_left, 1).start()

            if k == 1:

                @pl.when(b >= 1)
                def _():
                    z_wait(piece, 3)

                @pl.when((b >= 1) & (b < 3))
                def _():
                    z_copy(piece, 3, 2, z_right, 0).start()

                @pl.when(b <= 2)
                def _():
                    z_wait(piece, 1)

                @pl.when((b <= 2) & (b > 0))
                def _():
                    z_copy(piece, 1, 2, z_left, 1).start()

            if k == 2:
                z_wait(piece, 2)

                @pl.when(b == 2)
                def _():
                    z_copy(piece, 2, 1, z_right, 0).start()

                @pl.when(b == 1)
                def _():
                    z_copy(piece, 2, 3, z_left, 1).start()

            if k == 3:

                @pl.when(b == 0)
                def _():
                    z_wait(piece, 3)

                @pl.when(b == 3)
                def _():
                    z_wait(piece, 1)

    def squares_of(values):
        wide = values.astype(F32)
        return jnp.sum(wide * wide, 1, keepdims=True)

    def norms_j(k):
        for ref, norm in ((tj, norm_t), (sj, norm_s)):
            squares = squares_of(ref[slot(k)])
            norm[:, k * rows : (k + 1) * rows] = jnp.transpose(jnp.broadcast_to(squares, (rows, 128)))[0:8]

    def norms_i(at):
        for ref, norm in ((ti, own_t), (si, own_s)):
            own = ref[at]
            norm[at] = jnp.broadcast_to(squares_of(own), (own.shape[0], 128))

    def distance(ref, other, own_norm, norm, at, lo, hi):
        products = lax.dot_general(ref[at], other[lo:hi], NT, preferred_element_type=F32)
        spread = own_norm[at][:, 0:1] + norm[0:1, lo:hi] - 2.0 * products
        return jnp.sqrt(jnp.maximum(spread, 0.0) + 1.0)

    def distances(at, lo, hi, diagonal):
        near_t = distance(ti, tj, own_t, norm_t, at, lo, hi)
        near_s = distance(si, sj, own_s, norm_s, at, lo, hi)
        inverse = 1.0 / near_s
        if diagonal:
            row = lax.broadcasted_iota(jnp.int32, near_s.shape, 0)
            off = row != lax.broadcasted_iota(jnp.int32, near_s.shape, 1)
            near_t = jnp.where(off, near_t, 0.0)
            near_s = jnp.where(off, near_s, 0.0)
            inverse = jnp.where(off, inverse, 0.0)
        dist_t[at, lo:hi] = near_t
        dist_s[at, lo:hi] = near_s
        inv_s[at, lo:hi] = inverse
        return near_s, near_t

    def first_pass(k):
        norms_i(slot(k))
        times = 2.0 if 1 <= k <= 3 else 1.0
        return [times * fold(near) for near in distances(slot(k), 0, 3 * rows, k == 0)]

    def add(one, two):
        return [a + b for a, b in zip(one, two)]

    y_early(0)
    z_step(0)
    round_signal(0)
    y_early(1)
    round_wait(0)
    round_signal(1)
    y_early(2)
    z_step(1)
    round_wait(1)
    round_signal(2)
    y_early(3)
    y_late(0)
    norms_j(0)
    y_early(4)
    z_step(2)
    round_wait(2)
    norms_j(1)
    norms_j(2)
    total = first_pass(0)
    total = add(total, first_pass(1))
    y_late(1)
    total = add(total, first_pass(2))
    total = add(total, first_pass(3))
    y_late(2)
    total = add(total, first_pass(4))
    z_step(3)
    norms_j(3)

    def last_pass(start, count, times):
        near = distances(pl.ds(start * rows, count * rows), 3 * rows, 4 * rows, False)
        return [times * fold(one) for one in near]

    total = add(total, last_pass(0, 1, 1.0))
    total = add(total, last_pass(1, 3, 2.0))
    total = add(total, last_pass(4, 1, 1.0))

    def sum_all(which, pair, meanwhile):
        one, two = (jnp.sum(tile, 0, keepdims=True) for tile in pair)
        first = lax.broadcasted_iota(jnp.int32, (8, 128), 0) == 0
        tile = jnp.where(first, one, two)
        for stage, (where, me) in enumerate(stages):
            at = which * 3 + stage
            sums[at, me] = tile

            def copy(j, row):
                return pltpu.make_async_remote_copy(
                    src_ref=sums.at[at, row], dst_ref=sums.at[at, row],
                    send_sem=send_sum.at[at, j], recv_sem=recv_sum.at[at, row],
                    device_id=where(lax.rem(me + j, NP)), device_id_type=MESH,
                )

            for j in (4, 3, 5, 2, 6, 1, 7):
                copy(j, me).start()
            meanwhile[stage]()
            for j in range(1, NP):
                copy(j, lax.rem(me + j, NP)).wait_recv()
            tile = sums[at, 0]
            for j in range(1, NP):
                tile = tile + sums[at, j]
            for j in range(1, NP):
                copy(j, me).wait_send()
        wide = jnp.sum(tile, 1, keepdims=True)
        return wide[0:1], wide[1:2]

    def late_pass(k):
        norms_i(slot(k))
        distances(slot(k), 0, NZ * rows, False)

    def late_last():
        y_late(3)
        late_pass(5)

    def nothing():
        pass

    total_s, total_t = sum_all(0, total, (lambda: late_pass(7), lambda: late_pass(6), late_last))
    scale_s = pair_count / total_s
    scale_t = pair_count / total_t

    def second_pass(k, now):
        at = pl.ds(pl.multiple_of(k * rows, rows), rows)
        near_s = dist_s[at]
        error = near_s * scale_s - dist_t[at] * scale_t
        slope = jnp.clip(error, -1.0, 1.0)
        dist_t[at] = slope
        return now[0] + fold(slope * near_s), now[1] + fold(slope * (error - 0.5 * slope))

    zero = jnp.zeros((8, 128), F32)
    total = lax.fori_loop(1, 4, second_pass, (zero, zero))
    total = second_pass(0, second_pass(4, (2.0 * total[0], 2.0 * total[1])))

    def late_slopes():
        lax.fori_loop(5, NY, second_pass, (zero, zero))

    curvature, huber = sum_all(1, total, (late_slopes, nothing, nothing))
    loss_ref[...] = jnp.broadcast_to(huber / pair_count, (8, 128))
    factor = curvature * scale_s * scale_s / pair_count

    def third_pass(k, carry):
        start = pl.multiple_of(k * rows, rows)
        at = pl.ds(start, rows)
        weight = (dist_t[at] * scale_s - factor) * inv_s[at]
        w_ij[at] = weight.astype(jnp.bfloat16)
        w_ji[:, at] = jnp.transpose(weight).astype(jnp.bfloat16)
        return carry

    lax.fori_loop(0, NY, third_pass, 0)

    def make_i(k):
        weight = w_ij[slot(k)]
        count = jnp.sum(weight.astype(F32), 1, keepdims=True)
        part_i[slot(k)] = si[slot(k), cut:ds].astype(F32) * count - jnp.dot(
            weight, sj[:, cut:ds], preferred_element_type=F32
        )

    def make_j(k):
        at = pl.ds(pl.multiple_of(place(k, b) * rows, rows), rows)
        weight = w_ji[at]
        count = jnp.sum(weight.astype(F32), 1, keepdims=True)
        part_j[slot(k)] = sj[at, 0:cut].astype(F32) * count - jnp.dot(
            weight, si[:, 0:cut], preferred_element_type=F32
        )

    def gy_copy(way, m, piece):
        k = m if way == 0 else (NY - m) % NY
        return pltpu.make_async_remote_copy(
            src_ref=part_i.at[pl.ds(k * rows + piece * half, half)],
            dst_ref=(in_yr, in_yl)[way].at[m - 1, piece],
            send_sem=send_gy.at[way, m - 1, piece], recv_sem=recv_gy.at[way, m - 1, piece],
            device_id=(y_up, y_down)[way], device_id_type=MESH,
        )

    def gy_add(way, m, piece):
        gy_copy(way, m + 1, piece).wait_recv()
        k = m if way == 0 else (NY - m) % NY
        at = pl.ds(k * rows + piece * half, half)
        part_i[at] = part_i[at] + (in_yr, in_yl)[way][m, piece]

    def gz_copy(way, m, piece):
        k = m if way == 0 else (NZ - m) % NZ
        return pltpu.make_async_remote_copy(
            src_ref=part_j.at[pl.ds(k * rows + piece * half, half)],
            dst_ref=(in_zr, in_zl)[way].at[m - 1, piece],
            send_sem=send_gz.at[way, m - 1, piece], recv_sem=recv_gz.at[way, m - 1, piece],
            device_id=(z_right, z_left)[way], device_id_type=MESH,
        )

    def gz_add(way, m, piece):
        gz_copy(way, m + 1, piece).wait_recv()
        k = m if way == 0 else (NZ - m) % NZ
        at = pl.ds(k * rows + piece * half, half)
        part_j[at] = part_j[at] + (in_zr, in_zl)[way][m, piece]

    def gz_sends(way, m):
        sends = (b + m <= NZ - 1) if way == 0 else (b - m >= 0)
        comes = (b >= 1) if way == 0 else (b <= NZ - 2)
        return sends, sends & comes

    def gz_round(m, add):
        for piece in range(2):
            for way in range(2):
                sends, comes = gz_sends(way, m)
                if add:

                    @pl.when(comes)
                    def _():
                        gz_add(way, m, piece)

                @pl.when(sends)
                def _():
                    gz_copy(way, m, piece).start()

    make_i(4)
    gy_copy(0, 4, 0).start()
    gy_copy(1, 4, 1).start()
    make_j(3)
    make_j(1)
    gz_round(3, False)
    make_i(3)
    make_i(5)
    gy_copy(0, 3, 1).start()
    gy_copy(1, 3, 0).start()
    make_j(2)
    make_i(2)
    make_i(6)
    make_i(1)
    make_i(7)
    make_i(0)
    make_j(0)

    gy_add(0, 3, 0)
    gy_copy(0, 3, 0).start()
    gy_add(1, 3, 1)
    gy_copy(1, 3, 1).start()
    gz_round(2, True)
    for m in (2, 1):
        for piece in range(2):
            for way in range(2):
                order = 1 - piece if way == 0 else piece
                gy_add(way, m, order)
                gy_copy(way, m, order).start()
        if m == 2:
            gz_round(1, True)

    for piece in range(2):
        for way in range(2):
            sends, comes = gz_sends(way, 0)

            @pl.when(comes)
            def _():
                gz_add(way, 0, piece)

    for piece in range(2):
        for way in range(2):
            gy_add(way, 0, 1 - piece if way == 0 else piece)
    grad_ref[:, 0:cut] = part_j[0:rows]
    grad_ref[:, cut:ds] = part_i[0:rows]

    for piece in range(4):
        for k in range(4):
            y_copy(piece, k, k + 1, y_down).wait_send()
        for k in range(3):
            y_copy(piece, (NY - k) % NY, NY - k - 1, y_up).wait_send()
        for cond, src, dst, to, way in (
            (b < 3, 0, 3, z_right, 0), (b > 0, 0, 1, z_left, 1),
            ((b >= 1) & (b < 3), 3, 2, z_right, 0), ((b <= 2) & (b > 0), 1, 2, z_left, 1),
            (b == 2, 2, 1, z_right, 0), (b == 1, 2, 3, z_left, 1),
        ):

            @pl.when(cond)
            def _():
                z_copy(piece, src, dst, to, way).wait_send()

    for way in range(2):
        gy_copy(way, 4, way).wait_send()
        for m in (3, 2, 1):
            for piece in range(2):
                gy_copy(way, m, piece).wait_send()
            sends, _ = gz_sends(way, m)

            @pl.when(sends)
            def _():
                for piece in range(2):
                    gz_copy(way, m, piece).wait_send()


def shards(teacher, student):
    rows, dt = teacher.shape
    ds = student.shape[1]
    batch_rows = rows * lax.axis_size("blk")
    pair_count = 1.0 * lax.axis_size("group") * batch_rows * (batch_rows - 1)
    cut = ds // 2
    ni, nj = NY * rows, NZ * rows
    bf16 = jnp.bfloat16
    vmem, dma = pltpu.VMEM, pltpu.SemaphoreType.DMA
    gradient, loss = pl.pallas_call(
        functools.partial(kernel, pair_count),
        out_shape=(
            jax.ShapeDtypeStruct((rows, ds), F32),
            jax.ShapeDtypeStruct((8, 128), F32),
        ),
        in_specs=[pl.BlockSpec(memory_space=pltpu.HBM)] * 2,
        out_specs=[pl.BlockSpec(memory_space=vmem), pl.BlockSpec(memory_space=vmem)],
        scratch_shapes=[
            vmem((ni, dt), bf16), vmem((ni, ds), bf16), vmem((nj, dt), bf16), vmem((nj, ds), bf16),
            vmem((ni, nj), F32), vmem((ni, nj), F32), vmem((ni, nj), F32),
            vmem((8, nj), F32), vmem((8, nj), F32), vmem((ni, 128), F32), vmem((ni, 128), F32),
            vmem((ni, nj), bf16), vmem((nj, ni), bf16),
            vmem((ni, ds - cut), F32), vmem((nj, cut), F32),
            vmem((4, 2, rows // 2, ds - cut), F32), vmem((4, 2, rows // 2, ds - cut), F32),
            vmem((3, 2, rows // 2, cut), F32), vmem((3, 2, rows // 2, cut), F32),
            vmem((6, NP, 8, 128), F32),
            dma((4,)), dma((4, NY)), dma((4, NY)), dma((4, 2, NZ)), dma((4, NZ)),
            dma((6, NP)), dma((6, NP)),
            dma((2, 4, 2)), dma((2, 4, 2)), dma((2, 3, 2)), dma((2, 3, 2)),
            pltpu.SemaphoreType.REGULAR((3,)),
        ],
        compiler_params=pltpu.CompilerParams(
            collective_id=0, has_side_effects=True, vmem_limit_bytes=62 * 1024 * 1024
        ),
    )(teacher, student)
    return (gradient, loss[0, 0])


def solution(mesh):
    in_specs = (P(("group", "blk"), None), P(("group", "blk"), None))
    out_specs = (P(("group", "blk"), None), P())
    return jax.shard_map(shards, mesh=mesh, in_specs=in_specs, out_specs=out_specs, check_vma=False)
```

time: 109 us -> 103 us (0.945)
  the two profiles are of different devices: /device:TPU:16 before, /device:TPU:1 now
where the time goes in v2:
time: 103 us
  Pallas kernels  99.3 us (96%)
  local copies, waits for them, and re-layouts  2.95 us (3%)
    pallas_call x1, Pallas kernels, shards(): pl.pallas_call(functools.partial(kernel, pair_count), out_shape=(jax.Shap...  99.3 us

profile of v2, /device:TPU:1, one launch (start us, length us, event | category | flops | bytes accessed | tf_op | source)
XLA Modules:
  0.0 102.9 jit_solution(548387760801402486)
XLA Ops:
  0.6 99.3 %shard_map.41 = (f32[128,768]{1,0:T(8,128)}, f32[8,128]{1,0:T(8,128)}) custom-call(bf16[128,1024]{1,0:T(8,128)(2,1)} %t_ref.1, bf16[128,768]{1,0:T(8,128)(2,1)} %s_ref.1), custom_call_target="tpu_custom_call" | custom-call | tf_op jit(solution)/shard_map/pallas_call | solution.py:494
  100.0 1.2 %slice.3 = f32[1,1]{1,0:T(1,128)} slice(f32[8,128]{1,0:T(8,128)} %get-tuple-element.5), slice={[0:1], [0:1]} | slice | bytes 8 | tf_op jit(solution)/shard_map/slice | solution.py:520
  101.1 1.8 %copy.5 = f32[128,768]{1,0:T(8,128)} copy(f32[128,768]{1,0:T(8,128)} %get-tuple-element.8) | data formatting | bytes 786432

commit v3 on v2

--- a/solution.py
+++ b/solution.py
@@ -10,6 +10,7 @@
 F32 = jnp.float32
 NY = 8
 NZ = 4
+SPAN = 4096.0
 NX = 4
 NP = 8
 NT = (((1,), (1,)), ((), ()))
@@ -30,7 +31,7 @@
     ti, si, tj, sj,
     dist_t, dist_s, inv_s, norm_t, norm_s, own_t, own_s,
     w_ij, w_ji, part_i, part_j,
-    in_yr, in_yl, in_zr, in_zl,
+    out_y, out_z, in_y, in_z,
     sums,
     load, send_y, recv_y, send_z, recv_z,
     send_sum, recv_sum,
@@ -40,7 +41,7 @@
     rows = t_ref.shape[0]
     ds = s_ref.shape[1]
     half = rows // 2
-    cut = part_j.shape[1]
+    cut = part_j.shape[2]
     group = lax.axis_index("group")
     blk = lax.axis_index("blk")
     b, c = blk // NY, lax.rem(blk, NY)
@@ -304,97 +305,84 @@
         norms_i(slot(k))
         distances(slot(k), 0, NZ * rows, False)
 
-    def late_last():
-        y_late(3)
-        late_pass(5)
-
-    def nothing():
-        pass
-
-    total_s, total_t = sum_all(0, total, (lambda: late_pass(7), lambda: late_pass(6), late_last))
-    scale_s = pair_count / total_s
-    scale_t = pair_count / total_t
-
-    def second_pass(k, now):
-        at = pl.ds(pl.multiple_of(k * rows, rows), rows)
-        near_s = dist_s[at]
-        error = near_s * scale_s - dist_t[at] * scale_t
-        slope = jnp.clip(error, -1.0, 1.0)
-        dist_t[at] = slope
-        return now[0] + fold(slope * near_s), now[1] + fold(slope * (error - 0.5 * slope))
-
-    zero = jnp.zeros((8, 128), F32)
-    total = lax.fori_loop(1, 4, second_pass, (zero, zero))
-    total = second_pass(0, second_pass(4, (2.0 * total[0], 2.0 * total[1])))
-
-    def late_slopes():
-        lax.fori_loop(5, NY, second_pass, (zero, zero))
-
-    curvature, huber = sum_all(1, total, (late_slopes, nothing, nothing))
-    loss_ref[...] = jnp.broadcast_to(huber / pair_count, (8, 128))
-    factor = curvature * scale_s * scale_s / pair_count
-
-    def third_pass(k, carry):
-        start = pl.multiple_of(k * rows, rows)
-        at = pl.ds(start, rows)
-        weight = (dist_t[at] * scale_s - factor) * inv_s[at]
-        w_ij[at] = weight.astype(jnp.bfloat16)
-        w_ji[:, at] = jnp.transpose(weight).astype(jnp.bfloat16)
-        return carry
-
-    lax.fori_loop(0, NY, third_pass, 0)
-
-    def make_i(k):
+    def keep(k, weight):
+        w_ij[slot(k)] = weight.astype(jnp.bfloat16)
+        w_ji[:, k * rows : (k + 1) * rows] = jnp.transpose(weight).astype(jnp.bfloat16)
+
+    def make_i(set_, k):
         weight = w_ij[slot(k)]
         count = jnp.sum(weight.astype(F32), 1, keepdims=True)
-        part_i[slot(k)] = si[slot(k), cut:ds].astype(F32) * count - jnp.dot(
+        part_i[set_, slot(k)] = si[slot(k), cut:ds].astype(F32) * count - jnp.dot(
             weight, sj[:, cut:ds], preferred_element_type=F32
         )
 
-    def make_j(k):
+    def make_j(set_, k):
         at = pl.ds(pl.multiple_of(place(k, b) * rows, rows), rows)
         weight = w_ji[at]
         count = jnp.sum(weight.astype(F32), 1, keepdims=True)
-        part_j[slot(k)] = sj[at, 0:cut].astype(F32) * count - jnp.dot(
+        part_j[set_, slot(k)] = sj[at, 0:cut].astype(F32) * count - jnp.dot(
             weight, si[:, 0:cut], preferred_element_type=F32
         )
 
-    def gy_copy(way, m, piece):
-        k = m if way == 0 else (NY - m) % NY
+    def g_at(count, way, m, piece):
+        return pl.ds((m if way == 0 else (count - m) % count) * rows + piece * half, half)
+
+    def code(out, values):
+        width = values.shape[1]
+        largest = jnp.max(jnp.max(jnp.abs(values), 1, keepdims=True), 0, keepdims=True)
+        largest = jnp.maximum(largest, 1e-30).astype(jnp.bfloat16)
+        near = values * (SPAN / largest.astype(F32))
+        square = near * near
+        coded = (near * jnp.abs(near) * square * (square * square)).astype(jnp.bfloat16)
+        for n in range(width // 128):
+            out[n * half : (n + 1) * half] = coded[:, n * 128 : (n + 1) * 128]
+        out[half * (width // 128) :] = jnp.broadcast_to(largest, (16, 128))
+
+    def decode(ref, width):
+        blocks = [ref[n * half : (n + 1) * half] for n in range(width // 128)]
+        coded = jnp.concatenate(blocks, 1).astype(F32)
+        root = jnp.sqrt(jnp.sqrt(jnp.sqrt(jnp.abs(coded))))
+        scale = ref[half * (width // 128) :].astype(F32)[0:1, 0:1] * (1.0 / SPAN)
+        return jnp.where(coded < 0.0, -root, root) * scale
+
+    def gy_copy(set_, way, m, piece):
         return pltpu.make_async_remote_copy(
-            src_ref=part_i.at[pl.ds(k * rows + piece * half, half)],
-            dst_ref=(in_yr, in_yl)[way].at[m - 1, piece],
-            send_sem=send_gy.at[way, m - 1, piece], recv_sem=recv_gy.at[way, m - 1, piece],
+            src_ref=out_y.at[set_, way, m - 1, piece], dst_ref=in_y.at[set_, way, m - 1, piece],
+            send_sem=send_gy.at[set_, way, m - 1, piece], recv_sem=recv_gy.at[set_, way, m - 1, piece],
             device_id=(y_up, y_down)[way], device_id_type=MESH,
         )
 
-    def gy_add(way, m, piece):
-        gy_copy(way, m + 1, piece).wait_recv()
-        k = m if way == 0 else (NY - m) % NY
-        at = pl.ds(k * rows + piece * half, half)
-        part_i[at] = part_i[at] + (in_yr, in_yl)[way][m, piece]
-
-    def gz_copy(way, m, piece):
-        k = m if way == 0 else (NZ - m) % NZ
+    def gy_send(set_, way, m, piece):
+        code(out_y.at[set_, way, m - 1, piece], part_i[set_, g_at(NY, way, m, piece)])
+        gy_copy(set_, way, m, piece).start()
+
+    def gy_add(set_, way, m, piece):
+        gy_copy(set_, way, m + 1, piece).wait_recv()
+        at = g_at(NY, way, m, piece)
+        part_i[set_, at] = part_i[set_, at] + decode(in_y.at[set_, way, m, piece], ds - cut)
+
+    def gz_copy(set_, way, m, piece):
         return pltpu.make_async_remote_copy(
-            src_ref=part_j.at[pl.ds(k * rows + piece * half, half)],
-            dst_ref=(in_zr, in_zl)[way].at[m - 1, piece],
-            send_sem=send_gz.at[way, m - 1, piece], recv_sem=recv_gz.at[way, m - 1, piece],
+            src_ref=out_z.at[set_, way, m - 1, piece], dst_ref=in_z.at[set_, way, m - 1, piece],
+            send_sem=send_gz.at[set_, way, m - 1, piece], recv_sem=recv_gz.at[set_, way, m - 1, piece],
             device_id=(z_right, z_left)[way], device_id_type=MESH,
         )
 
-    def gz_add(way, m, piece):
-        gz_copy(way, m + 1, piece).wait_recv()
-        k = m if way == 0 else (NZ - m) % NZ
-        at = pl.ds(k * rows + piece * half, half)
-        part_j[at] = part_j[at] + (in_zr, in_zl)[way][m, piece]
+    def gz_send(set_, way, m, piece):
+        code(out_z.at[set_, way, m - 1, piece], part_j[set_, g_at(NZ, way, m, piece)])
+        gz_copy(set_, way, m, piece).start()
+
+    def gz_add(set_, way, m, piece):
+        gz_copy(set_, way, m + 1, piece).wait_recv()
+        at = g_at(NZ, way, m, piece)
+        part_j[set_, at] = part_j[set_, at] + decode(in_z.at[set_, way, m, piece], cut)
 
     def gz_sends(way, m):
         sends = (b + m <= NZ - 1) if way == 0 else (b - m >= 0)
         comes = (b >= 1) if way == 0 else (b <= NZ - 2)
         return sends, sends & comes
 
-    def gz_round(m, add):
+    def gz_round(set_, m, add):
         for piece in range(2):
             for way in range(2):
                 sends, comes = gz_sends(way, m)
@@ -402,57 +390,107 @@
 
                     @pl.when(comes)
                     def _():
-                        gz_add(way, m, piece)
-
-                @pl.when(sends)
-                def _():
-                    gz_copy(way, m, piece).start()
-
-    make_i(4)
-    gy_copy(0, 4, 0).start()
-    gy_copy(1, 4, 1).start()
-    make_j(3)
-    make_j(1)
-    gz_round(3, False)
-    make_i(3)
-    make_i(5)
-    gy_copy(0, 3, 1).start()
-    gy_copy(1, 3, 0).start()
-    make_j(2)
-    make_i(2)
-    make_i(6)
-    make_i(1)
-    make_i(7)
-    make_i(0)
-    make_j(0)
-
-    gy_add(0, 3, 0)
-    gy_copy(0, 3, 0).start()
-    gy_add(1, 3, 1)
-    gy_copy(1, 3, 1).start()
-    gz_round(2, True)
-    for m in (2, 1):
+                        gz_add(set_, way, m, piece)
+
+                if m > 0:
+
+                    @pl.when(sends)
+                    def _():
+                        gz_send(set_, way, m, piece)
+
+    def gy_round(set_, m):
         for piece in range(2):
             for way in range(2):
                 order = 1 - piece if way == 0 else piece
-                gy_add(way, m, order)
-                gy_copy(way, m, order).start()
-        if m == 2:
-            gz_round(1, True)
-
-    for piece in range(2):
-        for way in range(2):
-            sends, comes = gz_sends(way, 0)
-
-            @pl.when(comes)
-            def _():
-                gz_add(way, 0, piece)
-
-    for piece in range(2):
-        for way in range(2):
-            gy_add(way, 0, 1 - piece if way == 0 else piece)
-    grad_ref[:, 0:cut] = part_j[0:rows]
-    grad_ref[:, cut:ds] = part_i[0:rows]
+                gy_add(set_, way, m, order)
+                if m > 0:
+                    gy_send(set_, way, m, order)
+
+    def g_round(set_, number):
+        if number == 0:
+            make_i(set_, 4)
+            gy_send(set_, 0, 4, 0)
+            gy_send(set_, 1, 4, 1)
+            make_j(set_, 3)
+            make_j(set_, 1)
+            gz_round(set_, 3, False)
+            make_i(set_, 3)
+            make_i(set_, 5)
+            gy_send(set_, 0, 3, 1)
+            gy_send(set_, 1, 3, 0)
+            make_j(set_, 2)
+            for k in (2, 6, 1, 7, 0):
+                make_i(set_, k)
+            make_j(set_, 0)
+        if number == 1:
+            gy_add(set_, 0, 3, 0)
+            gy_send(set_, 0, 3, 0)
+            gy_add(set_, 1, 3, 1)
+            gy_send(set_, 1, 3, 1)
+            gz_round(set_, 2, True)
+        if number == 2:
+            gy_round(set_, 2)
+            gz_round(set_, 1, True)
+        if number == 3:
+            gy_round(set_, 1)
+        if number == 4:
+            gz_round(set_, 0, True)
+            gy_round(set_, 0)
+
+    def late_first():
+        late_pass(7)
+        late_pass(6)
+
+    def late_last():
+        y_late(3)
+        late_pass(5)
+
+    def inverse_parts():
+        for k in range(NY):
+            keep(k, inv_s[slot(k)])
+        g_round(0, 0)
+
+    total_s, total_t = sum_all(0, total, (late_first, late_last, inverse_parts))
+    scale_s = pair_count / total_s
+    scale_t = pair_count / total_t
+
+    def slope_of(k):
+        near_s = dist_s[slot(k)]
+        error = near_s * scale_s - dist_t[slot(k)] * scale_t
+        return near_s, error, jnp.clip(error, -1.0, 1.0)
+
+    def second_pass(k):
+        near_s, error, slope = slope_of(k)
+        dist_t[slot(k)] = slope
+        times = 2.0 if 1 <= k <= 3 else 1.0
+        return times * fold(slope * near_s), times * fold(slope * (error - 0.5 * slope))
+
+    total = second_pass(0)
+    for k in range(1, 5):
+        total = add(total, second_pass(k))
+
+    def slopes_first():
+        for k in range(NY):
+            keep(k, (dist_t[slot(k)] if k < 5 else slope_of(k)[2]) * inv_s[slot(k)])
+        g_round(1, 0)
+        g_round(0, 1)
+
+    def slopes_next():
+        g_round(0, 2)
+        g_round(1, 1)
+
+    def slopes_last():
+        g_round(0, 3)
+        g_round(1, 2)
+
+    curvature, huber = sum_all(1, total, (slopes_first, slopes_next, slopes_last))
+    loss_ref[...] = jnp.broadcast_to(huber / pair_count, (8, 128))
+    factor = curvature * scale_s * scale_s / pair_count
+    g_round(1, 3)
+    g_round(0, 4)
+    g_round(1, 4)
+    grad_ref[:, 0:cut] = scale_s * part_j[1, 0:rows] - factor * part_j[0, 0:rows]
+    grad_ref[:, cut:ds] = scale_s * part_i[1, 0:rows] - factor * part_i[0, 0:rows]
 
     for piece in range(4):
         for k in range(4):
@@ -469,17 +507,18 @@
             def _():
                 z_copy(piece, src, dst, to, way).wait_send()
 
-    for way in range(2):
-        gy_copy(way, 4, way).wait_send()
-        for m in (3, 2, 1):
-            for piece in range(2):
-                gy_copy(way, m, piece).wait_send()
-            sends, _ = gz_sends(way, m)
-
-            @pl.when(sends)
-            def _():
+    for set_ in range(2):
+        for way in range(2):
+            gy_copy(set_, way, 4, way).wait_send()
+            for m in (3, 2, 1):
                 for piece in range(2):
-                    gz_copy(way, m, piece).wait_send()
+                    gy_copy(set_, way, m, piece).wait_send()
+                sends, _ = gz_sends(way, m)
+
+                @pl.when(sends)
+                def _():
+                    for piece in range(2):
+                        gz_copy(set_, way, m, piece).wait_send()
 
 
 def shards(teacher, student):
@@ -490,6 +529,8 @@
     cut = ds // 2
     ni, nj = NY * rows, NZ * rows
     bf16 = jnp.bfloat16
+    y_parts = (2, 2, 4, 2, rows // 2 * (ds - cut) // 128 + 16, 128)
+    z_parts = (2, 2, 3, 2, rows // 2 * cut // 128 + 16, 128)
     vmem, dma = pltpu.VMEM, pltpu.SemaphoreType.DMA
     gradient, loss = pl.pallas_call(
         functools.partial(kernel, pair_count),
@@ -504,13 +545,12 @@
             vmem((ni, nj), F32), vmem((ni, nj), F32), vmem((ni, nj), F32),
             vmem((8, nj), F32), vmem((8, nj), F32), vmem((ni, 128), F32), vmem((ni, 128), F32),
             vmem((ni, nj), bf16), vmem((nj, ni), bf16),
-            vmem((ni, ds - cut), F32), vmem((nj, cut), F32),
-            vmem((4, 2, rows // 2, ds - cut), F32), vmem((4, 2, rows // 2, ds - cut), F32),
-            vmem((3, 2, rows // 2, cut), F32), vmem((3, 2, rows // 2, cut), F32),
+            vmem((2, ni, ds - cut), F32), vmem((2, nj, cut), F32),
+            vmem(y_parts, bf16), vmem(z_parts, bf16), vmem(y_parts, bf16), vmem(z_parts, bf16),
             vmem((6, NP, 8, 128), F32),
             dma((4,)), dma((4, NY)), dma((4, NY)), dma((4, 2, NZ)), dma((4, NZ)),
             dma((6, NP)), dma((6, NP)),
-            dma((2, 4, 2)), dma((2, 4, 2)), dma((2, 3, 2)), dma((2, 3, 2)),
+            dma((2, 2, 4, 2)), dma((2, 2, 4, 2)), dma((2, 2, 3, 2)), dma((2, 2, 3, 2)),
             pltpu.SemaphoreType.REGULAR((3,)),
         ],
         compiler_params=pltpu.CompilerParams(

time: 103 us -> 94.2 us (0.915)
  Pallas kernels: 99.3 us -> 89.6 us
    pallas_call x1, Pallas kernels: 99.3 us -> 89.6 us  [shards(): pl.pallas_call(functools.partial(kernel, pair_count), out_shape=(jax.Shap...]
where the time goes in v3:
time: 94.2 us; the launch traced here: 93.2 us
  Pallas kernels  89.6 us (95%)
  local copies, waits for them, and re-layouts  2.95 us (3%)
    pallas_call x1, Pallas kernels, shards(): pl.pallas_call(functools.partial(kernel, pair_count), out_shape=(jax.Shap...  89.6 us

profile of v3, /device:TPU:1, one launch (start us, length us, event | category | flops | bytes accessed | tf_op | source)
XLA Modules:
  0.0 93.2 jit_solution(9419407942742343651)
XLA Ops:
  0.6 89.6 %shard_map.41 = (f32[128,768]{1,0:T(8,128)}, f32[8,128]{1,0:T(8,128)}) custom-call(bf16[128,1024]{1,0:T(8,128)(2,1)} %t_ref.1, bf16[128,768]{1,0:T(8,128)(2,1)} %s_ref.1), custom_call_target="tpu_custom_call" | custom-call | tf_op jit(solution)/shard_map/pallas_call | solution.py:535
  90.3 1.2 %slice.3 = f32[1,1]{1,0:T(1,128)} slice(f32[8,128]{1,0:T(8,128)} %get-tuple-element.5), slice={[0:1], [0:1]} | slice | bytes 8 | tf_op jit(solution)/shard_map/slice | solution.py:560
  91.5 1.8 %copy.5 = f32[128,768]{1,0:T(8,128)} copy(f32[128,768]{1,0:T(8,128)} %get-tuple-element.8) | data formatting | bytes 786432

commit v4 on v3

--- a/solution.py
+++ b/solution.py
@@ -10,6 +10,7 @@
 F32 = jnp.float32
 NY = 8
 NZ = 4
+LATE = 12.0
 SPAN = 4096.0
 NX = 4
 NP = 8
@@ -31,7 +32,7 @@
     ti, si, tj, sj,
     dist_t, dist_s, inv_s, norm_t, norm_s, own_t, own_s,
     w_ij, w_ji, part_i, part_j,
-    out_y, out_z, in_y, in_z,
+    out_y, out_z, in_y, in_z, top_i, top_j,
     sums,
     load, send_y, recv_y, send_z, recv_z,
     send_sum, recv_sum,
@@ -61,7 +62,7 @@
     def xc_device(index):
         return device(z, index // 2, lax.rem(index, 2), c)
 
-    stages = ((y_device, c), (z_device, z), (xc_device, xc))
+    stages = ((z_device, z), (xc_device, xc), (y_device, c))
 
     y_right, y_left = y_device(lax.rem(c + 1, NY)), y_device(lax.rem(c + NY - 1, NY))
     z_right, z_left = z_device(lax.rem(z + 1, NP)), z_device(lax.rem(z + NP - 1, NP))
@@ -130,70 +131,67 @@
             device_id=z_right, device_id_type=MESH,
         ).wait_recv()
 
-    def y_early(k):
-        for piece in range(4):
-            if k > 0:
-                y_copy(piece, k - 1, k, y_down).wait_recv()
-            if k < 4:
-                y_copy(piece, k, k + 1, y_down).start()
-
-    def y_late(k):
-        for piece in range(4):
-            if k > 0:
-                y_copy(piece, (NY + 1 - k) % NY, NY - k, y_up).wait_recv()
-            if k < 3:
-                y_copy(piece, (NY - k) % NY, NY - k - 1, y_up).start()
-
-    def z_step(k):
-        for piece in range(4):
-            if k == 0:
-
-                @pl.when(b < 3)
-                def _():
-                    z_copy(piece, 0, 3, z_right, 0).start()
-
-                @pl.when(b > 0)
-                def _():
-                    z_copy(piece, 0, 1, z_left, 1).start()
-
-            if k == 1:
-
-                @pl.when(b >= 1)
-                def _():
-                    z_wait(piece, 3)
-
-                @pl.when((b >= 1) & (b < 3))
-                def _():
-                    z_copy(piece, 3, 2, z_right, 0).start()
-
-                @pl.when(b <= 2)
-                def _():
-                    z_wait(piece, 1)
-
-                @pl.when((b <= 2) & (b > 0))
-                def _():
-                    z_copy(piece, 1, 2, z_left, 1).start()
-
-            if k == 2:
-                z_wait(piece, 2)
-
-                @pl.when(b == 2)
-                def _():
-                    z_copy(piece, 2, 1, z_right, 0).start()
-
-                @pl.when(b == 1)
-                def _():
-                    z_copy(piece, 2, 3, z_left, 1).start()
-
-            if k == 3:
-
-                @pl.when(b == 0)
-                def _():
-                    z_wait(piece, 3)
-
-                @pl.when(b == 3)
-                def _():
-                    z_wait(piece, 1)
+    def y_early(k, piece):
+        if k > 0:
+            y_copy(piece, k - 1, k, y_down).wait_recv()
+        if k < 4:
+            y_copy(piece, k, k + 1, y_down).start()
+
+    def y_late(k, piece):
+        if k > 0:
+            y_copy(piece, (NY + 1 - k) % NY, NY - k, y_up).wait_recv()
+        if k < 3:
+            y_copy(piece, (NY - k) % NY, NY - k - 1, y_up).start()
+
+    def z_step(k, piece):
+        if k == 0:
+
+            @pl.when(b < 3)
+            def _():
+                z_copy(piece, 0, 3, z_right, 0).start()
+
+            @pl.when(b > 0)
+            def _():
+                z_copy(piece, 0, 1, z_left, 1).start()
+
+        if k == 1:
+
+            @pl.when(b >= 1)
+            def _():
+                z_wait(piece, 3)
+
+            @pl.when((b >= 1) & (b < 3))
+            def _():
+                z_copy(piece, 3, 2, z_right, 0).start()
+
+            @pl.when(b <= 2)
+            def _():
+                z_wait(piece, 1)
+
+            @pl.when((b <= 2) & (b > 0))
+            def _():
+                z_copy(piece, 1, 2, z_left, 1).start()
+
+        if k == 2:
+            z_wait(piece, 2)
+
+            @pl.when(b == 2)
+            def _():
+                z_copy(piece, 2, 1, z_right, 0).start()
+
+            @pl.when(b == 1)
+            def _():
+                z_copy(piece, 2, 3, z_left, 1).start()
+
+        if k == 3:
+
+            @pl.when(b == 0)
+            def _():
+                z_wait(piece, 3)
+
+            @pl.when(b == 3)
+            def _():
+                z_wait(piece, 1)
 
     def squares_of(values):
         wide = values.astype(F32)
@@ -230,39 +228,36 @@
         return near_s, near_t
 
     def first_pass(k):
-        norms_i(slot(k))
         times = 2.0 if 1 <= k <= 3 else 1.0
         return [times * fold(near) for near in distances(slot(k), 0, 3 * rows, k == 0)]
 
     def add(one, two):
         return [a + b for a, b in zip(one, two)]
 
-    y_early(0)
-    z_step(0)
-    round_signal(0)
-    y_early(1)
-    round_wait(0)
-    round_signal(1)
-    y_early(2)
-    z_step(1)
-    round_wait(1)
-    round_signal(2)
-    y_early(3)
-    y_late(0)
-    norms_j(0)
-    y_early(4)
-    z_step(2)
-    round_wait(2)
-    norms_j(1)
-    norms_j(2)
-    total = first_pass(0)
-    total = add(total, first_pass(1))
-    y_late(1)
-    total = add(total, first_pass(2))
-    total = add(total, first_pass(3))
-    y_late(2)
-    total = add(total, first_pass(4))
-    z_step(3)
+    total = [jnp.zeros((8, 128), F32)] * 2
+
+    def pass_now(k):
+        total[:] = add(total, first_pass(k))
+
+    def round_next(r):
+        round_wait(r)
+        if r < 2:
+            round_signal(r + 1)
+
+    steps = [(0.0, round_signal, (0,))]
+    for p in range(4):
+        steps += [(0.1 * p - 1.0, y_early, (0, p)), (0.1 * p - 0.95, z_step, (0, p))]
+        steps += [(2.6 + 4.6 * (k - 1) + 1.15 * (p + 1), y_early, (k, p)) for k in range(1, 5)]
+        steps += [(2.6 + 9.2 * (k - 1) + 2.3 * (p + 1), z_step, (k, p)) for k in range(1, 3)]
+        steps += [(90.0 + p, z_step, (3, p))]
+        steps += [(LATE + 0.01 * p, y_late, (0, p))]
+        steps += [(LATE + 2.6 + 4.6 * (k - 1) + 1.15 * (p + 1), y_late, (k, p)) for k in range(1, 3)]
+    steps += [(2.6 + 4.6 * k + 0.2, norms_i, (slot(k),)) for k in range(5)]
+    steps += [(0.1, norms_j, (0,)), (21.05, norms_j, (1,)), (21.1, norms_j, (2,))]
+    steps += [(21.2 + 1.2 * k, pass_now, (k,)) for k in range(4)] + [(29.0, pass_now, (4,))]
+    steps += [(7.5 + 4.0 * r, round_next, (r,)) for r in range(3)]
+    for _, step, args in sorted(steps, key=lambda one: one[0]):
+        step(*args)
     norms_j(3)
 
     def last_pass(start, count, times):
@@ -305,45 +300,60 @@
         norms_i(slot(k))
         distances(slot(k), 0, NZ * rows, False)
 
-    def keep(k, weight):
+    def keep(set_, k):
+        weight = inv_s[slot(k)]
+        if set_ == 1:
+            weight = weight * (dist_t[slot(k)] if k < 5 else slope_of(k)[2])
         w_ij[slot(k)] = weight.astype(jnp.bfloat16)
         w_ji[:, k * rows : (k + 1) * rows] = jnp.transpose(weight).astype(jnp.bfloat16)
 
     def make_i(set_, k):
         weight = w_ij[slot(k)]
         count = jnp.sum(weight.astype(F32), 1, keepdims=True)
-        part_i[set_, slot(k)] = si[slot(k), cut:ds].astype(F32) * count - jnp.dot(
+        part = si[slot(k), cut:ds].astype(F32) * count - jnp.dot(
             weight, sj[:, cut:ds], preferred_element_type=F32
         )
+        part_i[set_, slot(k)] = part
+        for piece in range(2):
+            top_i[set_, k, piece] = bound(part[piece * half : (piece + 1) * half])
 
     def make_j(set_, k):
         at = pl.ds(pl.multiple_of(place(k, b) * rows, rows), rows)
         weight = w_ji[at]
         count = jnp.sum(weight.astype(F32), 1, keepdims=True)
-        part_j[set_, slot(k)] = sj[at, 0:cut].astype(F32) * count - jnp.dot(
+        part = sj[at, 0:cut].astype(F32) * count - jnp.dot(
             weight, si[:, 0:cut], preferred_element_type=F32
         )
+        part_j[set_, slot(k)] = part
+        for piece in range(2):
+            top_j[set_, k, piece] = bound(part[piece * half : (piece + 1) * half])
 
     def g_at(count, way, m, piece):
         return pl.ds((m if way == 0 else (count - m) % count) * rows + piece * half, half)
 
-    def code(out, values):
+    def bound(values):
+        largest = jnp.max(jnp.max(jnp.abs(values), 1, keepdims=True), 0, keepdims=True)
+        return jnp.broadcast_to(jnp.maximum(largest, 1e-30), (8, 128))
+
+    def code(out, values, top):
+        scale = top[0:1].astype(jnp.bfloat16)
+        ratio = SPAN / scale.astype(F32)
         width = values.shape[1]
-        largest = jnp.max(jnp.max(jnp.abs(values), 1, keepdims=True), 0, keepdims=True)
-        largest = jnp.maximum(largest, 1e-30).astype(jnp.bfloat16)
-        near = values * (SPAN / largest.astype(F32))
-        square = near * near
-        coded = (near * jnp.abs(near) * square * (square * square)).astype(jnp.bfloat16)
         for n in range(width // 128):
-            out[n * half : (n + 1) * half] = coded[:, n * 128 : (n + 1) * 128]
-        out[half * (width // 128) :] = jnp.broadcast_to(largest, (16, 128))
+            near = values[:, n * 128 : (n + 1) * 128] * ratio
+            square = near * near
+            coded = near * jnp.abs(near) * square * (square * square)
+            out[n * half : (n + 1) * half] = coded.astype(jnp.bfloat16)
+        out[half * (width // 128) :] = jnp.broadcast_to(scale, (16, 128))
 
     def decode(ref, width):
-        blocks = [ref[n * half : (n + 1) * half] for n in range(width // 128)]
-        coded = jnp.concatenate(blocks, 1).astype(F32)
-        root = jnp.sqrt(jnp.sqrt(jnp.sqrt(jnp.abs(coded))))
-        scale = ref[half * (width // 128) :].astype(F32)[0:1, 0:1] * (1.0 / SPAN)
-        return jnp.where(coded < 0.0, -root, root) * scale
+        scale = ref[half * (width // 128) :].astype(F32)[0:8]
+        blocks = []
+        for n in range(width // 128):
+            coded = ref[n * half : (n + 1) * half].astype(F32)
+            root = jnp.sqrt(jnp.sqrt(jnp.sqrt(jnp.abs(coded)))) * (scale[0:1] * (1.0 / SPAN))
+            blocks.append(jnp.where(coded < 0.0, -root, root))
+        return jnp.concatenate(blocks, 1), scale
 
     def gy_copy(set_, way, m, piece):
         return pltpu.make_async_remote_copy(
@@ -353,13 +363,17 @@
         )
 
     def gy_send(set_, way, m, piece):
-        code(out_y.at[set_, way, m - 1, piece], part_i[set_, g_at(NY, way, m, piece)])
+        k = m if way == 0 else (NY - m) % NY
+        code(out_y.at[set_, way, m - 1, piece], part_i[set_, g_at(NY, way, m, piece)], top_i[set_, k, piece])
         gy_copy(set_, way, m, piece).start()
 
     def gy_add(set_, way, m, piece):
         gy_copy(set_, way, m + 1, piece).wait_recv()
         at = g_at(NY, way, m, piece)
-        part_i[set_, at] = part_i[set_, at] + decode(in_y.at[set_, way, m, piece], ds - cut)
+        k = m if way == 0 else (NY - m) % NY
+        values, scale = decode(in_y.at[set_, way, m, piece], ds - cut)
+        part_i[set_, at] = part_i[set_, at] + values
+        top_i[set_, k, piece] = top_i[set_, k, piece] + scale
 
     def gz_copy(set_, way, m, piece):
         return pltpu.make_async_remote_copy(
@@ -369,13 +383,17 @@
         )
 
     def gz_send(set_, way, m, piece):
-        code(out_z.at[set_, way, m - 1, piece], part_j[set_, g_at(NZ, way, m, piece)])
+        k = m if way == 0 else (NZ - m) % NZ
+        code(out_z.at[set_, way, m - 1, piece], part_j[set_, g_at(NZ, way, m, piece)], top_j[set_, k, piece])
         gz_copy(set_, way, m, piece).start()
 
     def gz_add(set_, way, m, piece):
         gz_copy(set_, way, m + 1, piece).wait_recv()
         at = g_at(NZ, way, m, piece)
-        part_j[set_, at] = part_j[set_, at] + decode(in_z.at[set_, way, m, piece], cut)
+        k = m if way == 0 else (NZ - m) % NZ
+        values, scale = decode(in_z.at[set_, way, m, piece], cut)
+        part_j[set_, at] = part_j[set_, at] + values
+        top_j[set_, k, piece] = top_j[set_, k, piece] + scale
 
     def gz_sends(way, m):
         sends = (b + m <= NZ - 1) if way == 0 else (b - m >= 0)
@@ -408,16 +426,20 @@
 
     def g_round(set_, number):
         if number == 0:
+            keep(set_, 4)
             make_i(set_, 4)
             gy_send(set_, 0, 4, 0)
             gy_send(set_, 1, 4, 1)
+            for k in (3, 5):
+                keep(set_, k)
+                make_i(set_, k)
+            gy_send(set_, 0, 3, 1)
+            gy_send(set_, 1, 3, 0)
+            for k in (2, 6, 1, 7, 0):
+                keep(set_, k)
             make_j(set_, 3)
             make_j(set_, 1)
             gz_round(set_, 3, False)
-            make_i(set_, 3)
-            make_i(set_, 5)
-            gy_send(set_, 0, 3, 1)
-            gy_send(set_, 1, 3, 0)
             make_j(set_, 2)
             for k in (2, 6, 1, 7, 0):
                 make_i(set_, k)
@@ -442,12 +464,11 @@
         late_pass(6)
 
     def late_last():
-        y_late(3)
+        for p in range(4):
+            y_late(3, p)
         late_pass(5)
 
     def inverse_parts():
-        for k in range(NY):
-            keep(k, inv_s[slot(k)])
         g_round(0, 0)
 
     total_s, total_t = sum_all(0, total, (late_first, late_last, inverse_parts))
@@ -470,23 +491,21 @@
         total = add(total, second_pass(k))
 
     def slopes_first():
-        for k in range(NY):
-            keep(k, (dist_t[slot(k)] if k < 5 else slope_of(k)[2]) * inv_s[slot(k)])
         g_round(1, 0)
         g_round(0, 1)
+        g_round(1, 1)
 
     def slopes_next():
         g_round(0, 2)
-        g_round(1, 1)
+        g_round(1, 2)
 
     def slopes_last():
         g_round(0, 3)
-        g_round(1, 2)
+        g_round(1, 3)
 
     curvature, huber = sum_all(1, total, (slopes_first, slopes_next, slopes_last))
     loss_ref[...] = jnp.broadcast_to(huber / pair_count, (8, 128))
     factor = curvature * scale_s * scale_s / pair_count
-    g_round(1, 3)
     g_round(0, 4)
     g_round(1, 4)
     grad_ref[:, 0:cut] = scale_s * part_j[1, 0:rows] - factor * part_j[0, 0:rows]
@@ -547,6 +566,7 @@
             vmem((ni, nj), bf16), vmem((nj, ni), bf16),
             vmem((2, ni, ds - cut), F32), vmem((2, nj, cut), F32),
             vmem(y_parts, bf16), vmem(z_parts, bf16), vmem(y_parts, bf16), vmem(z_parts, bf16),
+            vmem((2, NY, 2, 8, 128), F32), vmem((2, NZ, 2, 8, 128), F32),
             vmem((6, NP, 8, 128), F32),
             dma((4,)), dma((4, NY)), dma((4, NY)), dma((4, 2, NZ)), dma((4, NZ)),
             dma((6, NP)), dma((6, NP)),
@@ -554,7 +574,7 @@
             pltpu.SemaphoreType.REGULAR((3,)),
         ],
         compiler_params=pltpu.CompilerParams(
-            collective_id=0, has_side_effects=True, vmem_limit_bytes=62 * 1024 * 1024
+            collective_id=0, has_side_effects=True, vmem_limit_bytes=52 * 1024 * 1024
         ),
     )(teacher, student)
     return (gradient, loss[0, 0])

time: 94.2 us -> 87.4 us (0.928)
  Pallas kernels: 89.6 us -> 83.2 us
    pallas_call x1, Pallas kernels: 89.6 us -> 83.2 us  [shards(): pl.pallas_call(functools.partial(kernel, pair_count), out_shape=(jax.Shap...]
    unnamed x1 -> x5, local copies, waits for them, and re-layouts: 1.77 us -> 2.61 us
where the time goes in v4:
time: 87.4 us; the launch traced here: 87 us
  Pallas kernels  83.2 us (95%)
  local copies, waits for them, and re-layouts  3.13 us (4%)
    pallas_call x1, Pallas kernels, shards(): pl.pallas_call(functools.partial(kernel, pair_count), out_shape=(jax.Shap...  83.2 us
    unnamed x5, local copies, waits for them, and re-layouts  2.61 us

profile of v4, /device:TPU:1, one launch (start us, length us, event | category | flops | bytes accessed | tf_op | source)
XLA Modules:
  0.0 87.0 jit_solution(7256115165428690144)
XLA Ops:
  0.6 0.0 copy-start
  0.6 0.9 %copy-done = bf16[128,1024]{1,0:T(8,128)(2,1)S(1)} copy-done((bf16[128,1024]{1,0:T(8,128)(2,1)S(1)}, bf16[128,1024]{1,0:T(8,128)(2,1)}, u32[]{:S(2)}) %copy-start) | copy-done | bytes 262168
  1.6 0.0 copy-start.1
  1.6 0.9 %copy-done.1 = bf16[128,768]{1,0:T(8,128)(2,1)S(1)} copy-done((bf16[128,768]{1,0:T(8,128)(2,1)S(1)}, bf16[128,768]{1,0:T(8,128)(2,1)}, u32[]{:S(2)}) %copy-start.1) | copy-done | bytes 196632
  2.5 83.2 %shard_map.41 = (f32[128,768]{1,0:T(8,128)S(1)}, f32[8,128]{1,0:T(8,128)S(1)}) custom-call(bf16[128,1024]{1,0:T(8,128)(2,1)S(1)} %copy-done, bf16[128,768]{1,0:T(8,128)(2,1)S(1)} %copy-done.1), custom_call_target="tpu_custom_call" | custom-call | tf_op jit(solution)/shard_map/pallas_call | solution.py:554
  85.7 0.5 slice.3
  86.2 0.7 copy.5
Async XLA Ops:
  0.6 1.0 %copy-start = (bf16[128,1024]{1,0:T(8,128)(2,1)S(1)}, bf16[128,1024]{1,0:T(8,128)(2,1)}, u32[]{:S(2)}) copy-start(bf16[128,1024]{1,0:T(8,128)(2,1)} %t_ref.1) | copy-start | bytes 786436
  1.6 0.9 %copy-start.1 = (bf16[128,768]{1,0:T(8,128)(2,1)S(1)}, bf16[128,768]{1,0:T(8,128)(2,1)}, u32[]{:S(2)}) copy-start(bf16[128,768]{1,0:T(8,128)(2,1)} %s_ref.1) | copy-start | bytes 589828

commit v5 on v4

--- a/solution.py
+++ b/solution.py
@@ -85,8 +85,6 @@
     ]
     for copy in loads:
         copy.start()
-    for copy in loads:
-        copy.wait()
     pl.semaphore_wait(barrier, len(near))
 
     def round_signal(r):
@@ -104,7 +102,8 @@
 
     def y_copy(piece, src, dst, to):
         return pltpu.make_async_remote_copy(
-            src_ref=piece_of((si, ti), src, piece), dst_ref=piece_of((si, ti), dst, piece),
+            src_ref=piece_of((s_ref, t_ref) if src == 0 else (si, ti), src, piece),
+            dst_ref=piece_of((si, ti), dst, piece),
             send_sem=send_y.at[piece, dst], recv_sem=recv_y.at[piece, dst],
             device_id=to, device_id_type=MESH,
         )
@@ -119,7 +118,8 @@
 
     def z_copy(piece, src, dst, to, way):
         return pltpu.make_async_remote_copy(
-            src_ref=z_piece(src, b, piece), dst_ref=z_piece(dst, b + (1, -1)[way], piece),
+            src_ref=piece_of((s_ref, t_ref), 0, piece) if src == 0 else z_piece(src, b, piece),
+            dst_ref=z_piece(dst, b + (1, -1)[way], piece),
             send_sem=send_z.at[piece, way, dst], recv_sem=recv_z.at[piece, dst],
             device_id=to, device_id_type=MESH,
         )
@@ -244,7 +244,11 @@
         if r < 2:
             round_signal(r + 1)
 
-    steps = [(0.0, round_signal, (0,))]
+    def loaded():
+        for copy in loads:
+            copy.wait()
+
+    steps = [(0.0, round_signal, (0,)), (0.05, loaded, ())]
     for p in range(4):
         steps += [(0.1 * p - 1.0, y_early, (0, p)), (0.1 * p - 0.95, z_step, (0, p))]
         steps += [(2.6 + 4.6 * (k - 1) + 1.15 * (p + 1), y_early, (k, p)) for k in range(1, 5)]
@@ -481,10 +485,16 @@
         return near_s, error, jnp.clip(error, -1.0, 1.0)
 
     def second_pass(k):
-        near_s, error, slope = slope_of(k)
-        dist_t[slot(k)] = slope
         times = 2.0 if 1 <= k <= 3 else 1.0
-        return times * fold(slope * near_s), times * fold(slope * (error - 0.5 * slope))
+        sums_of = [jnp.zeros((8, 128), F32)] * 2
+        for n in range(NZ):
+            at = (slot(k), slice(n * 128, (n + 1) * 128))
+            near_s = dist_s[at]
+            error = near_s * scale_s - dist_t[at] * scale_t
+            slope = jnp.clip(error, -1.0, 1.0)
+            dist_t[at] = slope
+            sums_of = add(sums_of, (fold(slope * near_s), fold(slope * (error - 0.5 * slope))))
+        return [times * one for one in sums_of]
 
     total = second_pass(0)
     for k in range(1, 5):

time: 87.4 us -> 87.4 us (level)
  no operation moved by 1% of the time
where the time goes in v5:
time: 87.4 us; the launch traced here: 86.9 us
  Pallas kernels  83.1 us (95%)
  local copies, waits for them, and re-layouts  3.13 us (4%)
    pallas_call x1, Pallas kernels, shards(): pl.pallas_call(functools.partial(kernel, pair_count), out_shape=(jax.Shap...  83.1 us
    unnamed x5, local copies, waits for them, and re-layouts  2.61 us

profile of v5, /device:TPU:1, one launch (start us, length us, event | category | flops | bytes accessed | tf_op | source)
XLA Modules:
  0.0 86.9 jit_solution(2981543361294841826)
XLA Ops:
  0.6 0.0 copy-start
  0.6 0.9 %copy-done = bf16[128,1024]{1,0:T(8,128)(2,1)S(1)} copy-done((bf16[128,1024]{1,0:T(8,128)(2,1)S(1)}, bf16[128,1024]{1,0:T(8,128)(2,1)}, u32[]{:S(2)}) %copy-start) | copy-done | bytes 262168
  1.6 0.0 copy-start.1
  1.6 0.9 %copy-done.1 = bf16[128,768]{1,0:T(8,128)(2,1)S(1)} copy-done((bf16[128,768]{1,0:T(8,128)(2,1)S(1)}, bf16[128,768]{1,0:T(8,128)(2,1)}, u32[]{:S(2)}) %copy-start.1) | copy-done | bytes 196632
  2.5 83.1 %shard_map.41 = (f32[128,768]{1,0:T(8,128)S(1)}, f32[8,128]{1,0:T(8,128)S(1)}) custom-call(bf16[128,1024]{1,0:T(8,128)(2,1)S(1)} %copy-done, bf16[128,768]{1,0:T(8,128)(2,1)S(1)} %copy-done.1), custom_call_target="tpu_custom_call" | custom-call | tf_op jit(solution)/shard_map/pallas_call | solution.py:564
  85.6 0.5 slice.3
  86.1 0.7 copy.5
Async XLA Ops:
  0.6 1.0 %copy-start = (bf16[128,1024]{1,0:T(8,128)(2,1)S(1)}, bf16[128,1024]{1,0:T(8,128)(2,1)}, u32[]{:S(2)}) copy-start(bf16[128,1024]{1,0:T(8,128)(2,1)} %t_ref.1) | copy-start | bytes 786436
  1.6 0.9 %copy-start.1 = (bf16[128,768]{1,0:T(8,128)(2,1)S(1)}, bf16[128,768]{1,0:T(8,128)(2,1)}, u32[]{:S(2)}) copy-start(bf16[128,768]{1,0:T(8,128)(2,1)} %s_ref.1) | copy-start | bytes 589828
